TPU v7x, 32 devices: a whole 2x2x4 slice. The times are simulated.
32 devices in a mesh: pipe: 4 (over z), dp: 2 (over y), tensor: 4 (over x, core).
Axes of the slice: x: 2, y: 2, z: 4, core: 2. Of those that a mesh axis runs over, the one named last changes fastest.
Arguments:
- hidden_in: bfloat16 [8, 512, 8192], P(('pipe', 'dp'), None, 'tensor'), may hold values from -8 to 8
- norm_gain: bfloat16 [8192], P('tensor'), may hold values from 0.099609375 to 1.8984375
- queries: bfloat16 [8, 512, 8192], P(('pipe', 'dp'), None, 'tensor'), may hold values from -12 to 12
- key_weight: bfloat16 [8192, 1024], P('pipe', 'tensor'), may hold values from -1 to 1
- value_weight: bfloat16 [8192, 1024], P('pipe', 'tensor'), may hold values from -0.0625 to 0.0625
- out_grad: bfloat16 [8, 512, 8192], P(('pipe', 'dp'), None, 'tensor'), may hold values from -6 to 6
Outputs:
- attended: bfloat16 [8, 512, 8192], P(('pipe', 'dp'), None, 'tensor')
- key_grad: float32 [8192, 1024], P('pipe', 'tensor')
- value_grad: float32 [8192, 1024], P('pipe', 'tensor')
All inputs are finite; a program needn't handle non-finite values.
Results may differ from a plain program's by a relative error of at most 0.013.
The roundings to bfloat16 on the way count: a program that leaves them out, or rounds other values in their place, can miss the bound.
Values may be sent and summed in bfloat16 or wider, within the bound.
A program may use at most 128 MiB of HBM per device.

v0:
```python
import jax
import jax.numpy as jnp
from jax import lax
from jax.sharding import PartitionSpec as P

HD = 128
GROUP = 8


def shards(hidden_in, norm_gain, queries, key_weight, value_weight, out_grad):
    scale = 1.0 / HD**0.5
    whole, gain_full = (
        lax.all_gather(hidden_in, "tensor", axis=2, tiled=True),
        lax.all_gather(norm_gain, "tensor", axis=0, tiled=True),
    )
    wide = whole[0].astype(jnp.float32)
    power = jnp.mean(wide * wide, axis=-1, keepdims=True)
    normed = (wide * lax.rsqrt(power + 1e-05) * gain_full.astype(jnp.float32)).astype(jnp.bfloat16)
    tokens = normed.shape[0]
    kv_width = key_weight.shape[1]
    local_heads = kv_width // HD
    columns = normed
    key_sum = jnp.dot(
        columns,
        lax.all_gather(key_weight, "pipe", axis=0, tiled=True),
        preferred_element_type=jnp.float32,
    )
    value_sum = jnp.dot(
        columns,
        lax.all_gather(value_weight, "pipe", axis=0, tiled=True),
        preferred_element_type=jnp.float32,
    )
    keys = key_sum.astype(jnp.bfloat16).reshape(tokens, local_heads, HD)
    values = value_sum.astype(jnp.bfloat16).reshape(tokens, local_heads, HD)
    query_heads = queries[0].reshape(tokens, local_heads, GROUP, HD)
    grad_heads = out_grad[0].reshape(tokens, local_heads, GROUP, HD)
    scores = (
        jnp.einsum("qhgd,khd->hgqk", query_heads, keys, preferred_element_type=jnp.float32) * scale
    )
    position = jnp.arange(tokens, dtype=jnp.int32)
    visible = position[:, None] >= position[None, :]
    scores = jnp.where(visible, scores, -1e30)
    probs = jax.nn.softmax(scores, axis=-1)
    probs_low = probs.astype(jnp.bfloat16)
    attended = jnp.einsum("hgqk,khd->qhgd", probs_low, values, preferred_element_type=jnp.float32)
    attended = attended.reshape(1, tokens, local_heads * GROUP * HD).astype(jnp.bfloat16)
    dprobs = jnp.einsum("qhgd,khd->hgqk", grad_heads, values, preferred_element_type=jnp.float32)
    inner = jnp.sum(dprobs * probs, axis=-1, keepdims=True)
    dscores = (probs * (dprobs - inner) * scale).astype(jnp.bfloat16)
    dvalues = jnp.einsum(
        "hgqk,qhgd->khd", probs_low, grad_heads, preferred_element_type=jnp.float32
    )
    dkeys = jnp.einsum("hgqk,qhgd->khd", dscores, query_heads, preferred_element_type=jnp.float32)
    combined = jnp.concatenate(
        [
            dkeys.reshape(tokens, kv_width).astype(jnp.bfloat16),
            dvalues.reshape(tokens, kv_width).astype(jnp.bfloat16),
        ],
        axis=1,
    )
    columns = normed
    partial_sum = lax.psum_scatter(
        lax.dot_general(
            columns, combined, (((0,), (0,)), ((), ())), preferred_element_type=jnp.float32
        ),
        "pipe",
        scatter_dimension=0,
        tiled=True,
    )
    total = lax.psum(partial_sum, "dp")
    return (attended, total[:, :kv_width], total[:, kv_width:])


def solution(mesh):
    placed = (
        P(("pipe", "dp"), None, "tensor"),
        P("tensor"),
        P(("pipe", "dp"), None, "tensor"),
        P("pipe", "tensor"),
        P("pipe", "tensor"),
        P(("pipe", "dp"), None, "tensor"),
    )
    return jax.shard_map(
        shards,
        mesh=mesh,
        in_specs=placed,
        out_specs=(P(("pipe", "dp"), None, "tensor"), P("pipe", "tensor"), P("pipe", "tensor")),
        check_vma=False,
    )
```

profile of v0, /device:TPU:24, one launch (start us, length us, event | category | flops | bytes accessed | tf_op | source)
XLA Modules:
  0.0 696.2 jit_solution(2125509696893140490)
XLA Ops:
  7.2 0.7 all-gather.4.cloned.1.call-update
  7.9 0.7 all-gather.6.cloned.1.call-update
  8.7 0.7 all-gather.8.cloned.1.call-update
  9.4 5.3 all_gather.13
  14.8 4.0 copy.41
  18.7 3.1 copy.42
  21.8 0.1 iota_compare_fusion
  21.9 47.0 %all-gather.4.cloned.1.call-done = bf16[1,512,8192]{2,1,0:T(8,128)(2,1)} async-done(((bf16[1,512,2048]{2,1,0:T(8,128)(2,1)}), bf16[1,512,8192]{2,1,0:T(8,128)(2,1)}) %all-gather.4.cloned.1.call-update) | async-done | bytes 8388624 | tf_op jit(solution)/shard_map/all_gather | solution.py:13
  68.9 5.1 fusion.2
  74.0 74.5 %all-gather.6.cloned.1.call-done = bf16[8192,256]{1,0:T(8,128)(2,1)} async-done(((bf16[2048,256]{1,0:T(8,128)(2,1)}), bf16[8192,256]{1,0:T(8,128)(2,1)}) %all-gather.6.cloned.1.call-update) | async-done | bytes 4194320 | tf_op jit(solution)/shard_map/all_gather | solution.py:30
  148.5 7.4 %convolution_convert_fusion.1 = bf16[512,256]{0,1:T(8,128)(2,1)S(1)} fusion(bf16[8192,256]{1,0:T(8,128)(2,1)} %all-gather.6.cloned.1.call-done, bf16[1,512,8192]{2,1,0:T(8,128)(2,1)} %all-gather.4.cloned.1.call-done, f32[8192]{0:T(1024)S(1)} %convert_element_type.61, f32[512]{0:T(512)S(1)} %add_rsqrt_fusion), kind=kOutput, calls=%fused_computation.32 | convolution fusion | flops 2164391936 | bytes 12879872 | tf_op jit(solution)/shard_map/dot_general | solution.py:28
  155.9 8.7 %fusion.50 = f32[2,512,512,8]{2,1,3,0:T(8,128)} fusion(bf16[512,2,128,1]{0,2,3,1:T(8,128)(2,1)S(1)} %bitcast.90, bf16[512,2,8,128]{0,3,2,1:T(8,128)(2,1)S(1)} %bitcast.85), kind=kOutput, calls=%fused_computation.46 | convolution fusion | flops 1073741824 | bytes 19136512 | tf_op jit(solution)/shard_map/qhgd,khd->hgqk/dot_general | solution.py:47
  164.6 64.8 %all-gather.8.cloned.1.call-done = bf16[8192,256]{1,0:T(8,128)(2,1)} async-done(((bf16[2048,256]{1,0:T(8,128)(2,1)}), bf16[8192,256]{1,0:T(8,128)(2,1)}) %all-gather.8.cloned.1.call-update) | async-done | bytes 4194320 | tf_op jit(solution)/shard_map/all_gather | solution.py:25
  229.4 7.4 %convolution_convert_fusion = bf16[512,256]{0,1:T(8,128)(2,1)S(1)} fusion(bf16[8192,256]{1,0:T(8,128)(2,1)} %all-gather.8.cloned.1.call-done, bf16[1,512,8192]{2,1,0:T(8,128)(2,1)} %all-gather.4.cloned.1.call-done, f32[8192]{0:T(1024)S(1)} %convert_element_type.61, f32[512]{0:T(512)S(1)} %add_rsqrt_fusion), kind=kOutput, calls=%fused_computation.31 | convolution fusion | flops 2164391936 | bytes 12879872 | tf_op jit(solution)/shard_map/dot_general | solution.py:23
  236.8 11.0 %fusion.49 = (f32[2,8,512]{2,1,0:T(8,128)S(1)}, f32[2,8,512,512]{2,3,1,0:T(8,128)}) fusion(pred[512,512]{0,1:T(8,128)(4,1)S(1)} %iota_compare_fusion, bf16[512,2,128,1]{0,2,3,1:T(8,128)(2,1)S(1)} %bitcast.94, bf16[512,2,8,128]{0,3,2,1:T(8,128)(2,1)} %bitcast.87), kind=kOutput, calls=%fused_computation.45 | convolution fusion | flops 1090519552 | bytes 19431424 | tf_op jit(solution)/shard_map/sub | solution.py:43
  247.8 8.6 %fusion.30 = bf16[2,512,128]{1,2,0:T(8,128)(2,1)S(1)} fusion(bf16[512,2,8,128]{0,3,2,1:T(8,128)(2,1)S(1)} %bitcast.86, f32[2,8,512,512]{2,3,1,0:T(8,128)} %get-tuple-element.12, f32[2,8,512]{2,1,0:T(8,128)S(1)} %get-tuple-element.11), kind=kOutput, calls=%fused_computation.29 | convolution fusion | flops 1082261504 | bytes 19169280 | tf_op jit(solution)/shard_map/hgqk,qhgd->khd/dot_general | solution.py:50
  256.4 22.6 %fusion.33 = bf16[2,512,128]{1,2,0:T(8,128)(2,1)S(1)} fusion(bf16[512,2,8,128]{0,3,2,1:T(8,128)(2,1)} %bitcast.88, f32[2,512,512,8]{2,1,3,0:T(8,128)} %fusion.50, f32[2,8,512,512]{2,3,1,0:T(8,128)} %get-tuple-element.12, f32[2,8,512]{2,1,0:T(8,128)S(1)} %get-tuple-element.11), kind=kOutput, calls=%fused_computation.30 | convolution fusion | flops 1103241728 | bytes 35946496 | tf_op jit(solution)/shard_map/hgqk,qhgd->khd/dot_general | solution.py:53
  279.0 13.3 %fusion.36 = f32[8192,512]{1,0:T(8,128)} fusion(bf16[512,256]{0,1:T(8,128)(2,1)S(1)} %bitcast.92, bf16[512,256]{0,1:T(8,128)(2,1)S(1)} %bitcast.93, bf16[1,512,8192]{2,1,0:T(8,128)(2,1)} %all-gather.4.cloned.1.call-done, f32[8192]{0:T(1024)S(1)} %convert_element_type.61, f32[512]{0:T(512)S(1)} %add_rsqrt_fusion), kind=kOutput, calls=%fused_computation.34 | convolution fusion | flops 4312793088 | bytes 25724928 | tf_op jit(solution)/shard_map/dot_general | solution.py:63
  292.4 0.0 all-reduce.2.cloned.1.call-start
  292.5 281.2 %reduce-scatter.2.cloned.1.call-done = f32[2048,512]{1,0:T(8,128)} async-done(((f32[8192,512]{1,0:T(8,128)}), f32[2048,512]{1,0:T(8,128)}) %reduce-scatter.2.cloned.1.call-update) | async-done | bytes 4194320 | tf_op jit(solution)/shard_map/reduce_scatter | solution.py:62
  573.6 7.1 %fusion.19 = bf16[2,128,8,512]{3,1,2,0:T(8,128)(2,1)S(1)} fusion(bf16[512,2,128,1]{0,2,3,1:T(8,128)(2,1)S(1)} %bitcast.91, f32[2,8,512,512]{2,3,1,0:T(8,128)} %get-tuple-element.12, f32[2,8,512]{2,1,0:T(8,128)S(1)} %get-tuple-element.11), kind=kOutput, calls=%fused_computation.25 | convolution fusion | flops 1083179008 | bytes 19169280 | tf_op jit(solution)/shard_map/hgqk,khd->qhgd/dot_general | solution.py:45
  580.7 2.4 copy.28
  583.1 102.1 %all-reduce.2.cloned.1.call-done = f32[2048,512]{1,0:T(8,128)} async-done(((f32[2048,512]{1,0:T(8,128)}), f32[2048,512]{1,0:T(8,128)}) %all-reduce.2.cloned.1.call-update) | async-done | bytes 4194320 | tf_op jit(solution)/shard_map/psum | solution.py:70
  685.2 4.5 fusion.48
  (8 shorter events, 0.2 us)
Async XLA Ops:
  7.2 61.7 %all-gather.4.cloned.1.call-start = ((), (), s32[]{:S(2)}) async-start(), calls=%async_computation.1 | async-start | bytes 10485760 | tf_op jit(solution)/shard_map/all_gather | solution.py:13
  7.9 140.6 %all-gather.6.cloned.1.call-start = ((), (), s32[]{:S(2)}) async-start(), calls=%async_computation.2 | async-start | bytes 5242880 | tf_op jit(solution)/shard_map/all_gather | solution.py:30
  8.6 220.7 %all-gather.8.cloned.1.call-start = ((), (), s32[]{:S(2)}) async-start(), calls=%async_computation.3 | async-start | bytes 5242880 | tf_op jit(solution)/shard_map/all_gather | solution.py:25
  9.4 564.2 %reduce-scatter.2.cloned.1.call-start = ((), (), s32[]{:S(2)}) async-start(), calls=%async_computation.4 | async-start | bytes 20971520 | tf_op jit(solution)/shard_map/reduce_scatter | solution.py:62
  292.4 392.8 %all-reduce.2.cloned.1.call-start = ((), (), s32[]{:S(2)}) async-start(), calls=%async_computation.5 | async-start | bytes 8388608 | tf_op jit(solution)/shard_map/psum | solution.py:70
Sparse Core Ops, SparseCore 0:
  9.6 59.2 all-gather.3
  70.4 78.0 all-gather.5
  150.1 79.2 all-gather.7
  292.5 281.0 reduce-scatter.1
  576.0 109.0 all-reduce.1
where the time goes:
time: 698 us; the launch traced here: 696 us
  waiting for transfers between devices  572 us (82%)
  matrix products  86.2 us (12%)
  local copies, waits for them, and re-layouts  13.9 us (2%)
  between operations  13.8 us (2%)
    reduce_scatter x1, waiting for transfers between devices, shards(): lax.psum_scatter(lax.dot_general(columns, combined, (((0,), (0,)), ((), (...  281 us
    psum x1, waiting for transfers between devices, shards(): total = lax.psum(partial_sum, 'dp')  102 us
    all_gather x1, waiting for transfers between devices, shards(): lax.all_gather(value_weight, 'pipe', axis=0, tiled=True)  74.5 us
    all_gather x1, waiting for transfers between devices, shards(): lax.all_gather(key_weight, 'pipe', axis=0, tiled=True)  64.8 us
    all_gather x1, waiting for transfers between devices, shards(): lax.all_gather(hidden_in, 'tensor', axis=2, tiled=True)  47 us
    dot_general x1, matrix products, shards(): jnp.einsum('hgqk,qhgd->khd', dscores, query_heads, preferred_element_type...  22.6 us
  transfers between devices with their start and end apart: 5, of which 5 were waited for; matrix products, arithmetic and copies ran while one was open for 5% of the time, Pallas kernels for 0%

commit v1 on v0

v1 whole, which is shorter than its diff:
```python
import functools
import jax
import jax.numpy as jnp
from jax import lax
from jax.experimental import pallas as pl
from jax.experimental.pallas import tpu as pltpu
from jax.sharding import PartitionSpec as P

HD = 128
GROUP = 8
MESH = pl.DeviceIdType.MESH


def gather_kernel(
    n, hc, wc, h_in, g_in, k_in, v_in, h_out, g_out, k_out, v_out,
    loc_sem, hx_s, hx_r, hs_s, hs_r, hf_s, hf_r, g_s, g_r, zu_s, zd_s, z_r, y_s, y_r,
):
    p = lax.axis_index("pipe")
    d = lax.axis_index("dp")
    t = lax.axis_index("tensor")
    a, c = t // 2, t % 2
    across, sibling = (1 - a) * 2 + c, a * 2 + (1 - c)
    far = (1 - a) * 2 + (1 - c)
    rows, width = h_in.shape
    depth = k_in.shape[0]
    half = depth // 2
    piece = half // wc
    hrows = rows // hc

    barrier = pltpu.get_barrier_semaphore()
    for peer in (across, sibling, far):
        pl.semaphore_signal(barrier, inc=1, device_id=(p, d, peer), device_id_type=MESH)
    pl.semaphore_signal(barrier, inc=1, device_id=(p, 1 - d, t), device_id_type=MESH)

    for peer in (lax.rem(p + 1, n), lax.rem(p + n - 1, n)):
        pl.semaphore_signal(barrier, inc=1, device_id=(peer, d, t), device_id_type=MESH)
    pl.semaphore_wait(barrier, 6)

    def remote(src, dst, ssem, rsem, dev):
        return pltpu.make_async_remote_copy(
            src_ref=src, dst_ref=dst, send_sem=ssem, recv_sem=rsem, device_id=dev, device_id_type=MESH
        )

    def cols(i):
        return pl.ds(pl.multiple_of(i * width, width), width)

    def hslice(ref, i, k):
        return ref.at[pl.ds(k * hrows, hrows), cols(i)]

    def hown(k):
        return h_in.at[pl.ds(k * hrows, hrows)]

    def x_copy(k, owner):
        return remote(hown(k), hslice(h_out, owner, k), hx_s.at[k], hx_r.at[k], (p, d, across))

    def sib_copy(k, owner):
        return remote(hown(k), hslice(h_out, owner, k), hs_s.at[k], hs_r.at[k], (p, d, sibling))

    def fwd_copy(k, owner):
        return remote(
            hslice(h_out, owner, k), hslice(h_out, owner, k), hf_s.at[k], hf_r.at[k], (p, d, sibling)
        )

    def wpart(ref, b, k, hd):
        return ref.at[b, pl.ds(hd * half + (k % wc) * piece, piece)]

    def wout(k):
        return k_out if k < wc else v_out

    def wsrc(k):
        return (k_in if k < wc else v_in).at[pl.ds(d * half + (k % wc) * piece, piece)]

    def z_copy(src, b, k, up):
        dev = (p + 1, d, t) if up else (p - 1, d, t)
        sem = zu_s if up else zd_s
        return remote(src, wpart(wout(k), b, k, d), sem.at[b, k], z_r.at[b, k], dev)

    def y_copy(b, k, hd):
        part = wpart(wout(k), b, k, hd)
        return remote(part, part, y_s.at[b, k], y_r.at[b, k], (p, 1 - d, t))

    for k in range(2 * wc):

        @pl.when(p < n - 1)
        def _(k=k):
            z_copy(wsrc(k), p, k, True).start()

        @pl.when(p > 0)
        def _(k=k):
            z_copy(wsrc(k), p, k, False).start()

    gains = [
        remote(g_in, g_out.at[t], g_s.at[i], g_r.at[i], (p, d, peer))
        for i, peer in enumerate((across, sibling, far))
    ]
    for copy in gains:
        copy.start()
    for k in range(hc):
        x_copy(k, t).start()
    for k in range(hc):
        sib_copy(k, t).start()
    local = [
        pltpu.make_async_copy(h_in, h_out.at[:, cols(t)], loc_sem.at[0]),
        pltpu.make_async_copy(g_in, g_out.at[t], loc_sem.at[1]),
        pltpu.make_async_copy(k_in, k_out.at[p], loc_sem.at[2]),
        pltpu.make_async_copy(v_in, v_out.at[p], loc_sem.at[3]),
    ]
    for copy in local:
        copy.start()

    def hidden_step(k):
        x_copy(k, across).wait_recv()
        fwd_copy(k, across).start()

    done = 0
    for s in range(1, n):
        for k in range(2 * wc):

            @pl.when(p - s >= 0)
            def _(s=s, k=k):
                b = p - s
                z_copy(wsrc(k), b, k, True).wait_recv()

                @pl.when(p < n - 1)
                def _():
                    z_copy(wpart(wout(k), b, k, d), b, k, True).start()

                y_copy(b, k, d).start()

            @pl.when(p + s < n)
            def _(s=s, k=k):
                b = p + s
                z_copy(wsrc(k), b, k, False).wait_recv()

                @pl.when(p > 0)
                def _():
                    z_copy(wpart(wout(k), b, k, d), b, k, False).start()

                y_copy(b, k, d).start()

        goal = hc if s == n - 1 else min(hc, (hc * s) // (n - 1))
        while done < goal:
            hidden_step(done)
            done += 1

    for s in range(1, n):
        for k in range(2 * wc):
            for up in (True, False):
                b = p - s if up else p + s

                @pl.when((b >= 0) & (b < n))
                def _(b=b, k=k):
                    y_copy(b, k, 1 - d).wait_recv()
                    y_copy(b, k, d).wait_send()

    for s in range(n):
        for k in range(2 * wc):

            @pl.when((p - s >= 0) & (p < n - 1))
            def _(s=s, k=k):
                z_copy(wsrc(k), p - s, k, True).wait_send()

            @pl.when((p + s < n) & (p > 0))
            def _(s=s, k=k):
                z_copy(wsrc(k), p + s, k, False).wait_send()

    for k in range(hc):
        sib_copy(k, sibling).wait_recv()
        fwd_copy(k, far).wait_recv()
        x_copy(k, t).wait_send()
        sib_copy(k, t).wait_send()
        fwd_copy(k, across).wait_send()
    for i, peer in enumerate((across, sibling, far)):
        remote(g_in, g_out.at[peer], g_s.at[i], g_r.at[i], (p, d, peer)).wait_recv()
    for copy in gains:
        copy.wait_send()
    for copy in local:
        copy.wait()


def gather_all(n, hidden, gain, key_weight, value_weight):
    rows, width = hidden.shape
    depth, kv = key_weight.shape
    gain = gain.reshape(-1, 128)
    hc = 4
    wc = 2 if n <= 8 else 1
    dma = pltpu.SemaphoreType.DMA
    any_spec = pl.BlockSpec(memory_space=pl.ANY)
    return pl.pallas_call(
        functools.partial(gather_kernel, n, hc, wc),
        out_shape=[
            jax.ShapeDtypeStruct((rows, 4 * width), hidden.dtype),
            jax.ShapeDtypeStruct((4,) + gain.shape, gain.dtype),
            jax.ShapeDtypeStruct((n, depth, kv), key_weight.dtype),
            jax.ShapeDtypeStruct((n, depth, kv), value_weight.dtype),
        ],
        in_specs=[any_spec] * 4,
        out_specs=[any_spec] * 4,
        scratch_shapes=[
            dma((4,)),
            dma((hc,)), dma((hc,)), dma((hc,)), dma((hc,)), dma((hc,)), dma((hc,)),
            dma((3,)), dma((3,)),
            dma((n, 2 * wc)), dma((n, 2 * wc)), dma((n, 2 * wc)), dma((n, 2 * wc)), dma((n, 2 * wc)),
        ],
        compiler_params=pltpu.CompilerParams(collective_id=0, has_side_effects=True),
        name="gather_inputs",
    )(hidden, gain, key_weight, value_weight)


def shards(n, hidden_in, norm_gain, queries, key_weight, value_weight, out_grad):
    scale = 1.0 / HD**0.5
    pipe = lax.axis_index("pipe")
    tensor = lax.axis_index("tensor")
    depth, kv_width = key_weight.shape
    whole, gains, all_key, all_value = gather_all(n, hidden_in[0], norm_gain, key_weight, value_weight)
    wide = whole.astype(jnp.float32)
    power = jnp.mean(wide * wide, axis=-1, keepdims=True)
    normed = (wide * lax.rsqrt(power + 1e-05) * gains.reshape(-1).astype(jnp.float32)).astype(jnp.bfloat16)
    tokens = normed.shape[0]
    local_heads = kv_width // HD

    quarter = tokens // 4
    mine = lax.dynamic_slice_in_dim(normed, tensor * quarter, quarter, 0)
    parts = []
    for s in range(n):
        dest = lax.rem(pipe + s, n)
        block = lax.dynamic_slice_in_dim(mine, dest * depth, depth, 1)
        if s:
            block = lax.ppermute(block, "pipe", [(i, (i + s) % n) for i in range(n)])
        parts.append(block)
    columns = lax.all_gather(jnp.stack(parts), "tensor", axis=0)

    keys = jnp.dot(normed, all_key.reshape(-1, kv_width), preferred_element_type=jnp.float32)
    values = jnp.dot(normed, all_value.reshape(-1, kv_width), preferred_element_type=jnp.float32)
    keys = keys.astype(jnp.bfloat16).reshape(tokens, local_heads, HD)
    values = values.astype(jnp.bfloat16).reshape(tokens, local_heads, HD)
    query_heads = queries[0].reshape(tokens, local_heads, GROUP, HD)
    grad_heads = out_grad[0].reshape(tokens, local_heads, GROUP, HD)
    scores = (
        jnp.einsum("qhgd,khd->hgqk", query_heads, keys, preferred_element_type=jnp.float32) * scale
    )
    position = jnp.arange(tokens, dtype=jnp.int32)
    visible = position[:, None] >= position[None, :]
    scores = jnp.where(visible, scores, -1e30)
    probs = jax.nn.softmax(scores, axis=-1)
    probs_low = probs.astype(jnp.bfloat16)
    attended = jnp.einsum("hgqk,khd->qhgd", probs_low, values, preferred_element_type=jnp.float32)
    attended = attended.reshape(1, tokens, local_heads * GROUP * HD).astype(jnp.bfloat16)
    dprobs = jnp.einsum("qhgd,khd->hgqk", grad_heads, values, preferred_element_type=jnp.float32)
    inner = jnp.sum(dprobs * probs, axis=-1, keepdims=True)
    dscores = (probs * (dprobs - inner) * scale).astype(jnp.bfloat16)
    dvalues = jnp.einsum(
        "hgqk,qhgd->khd", probs_low, grad_heads, preferred_element_type=jnp.float32
    )
    dkeys = jnp.einsum("hgqk,qhgd->khd", dscores, query_heads, preferred_element_type=jnp.float32)
    combined = jnp.concatenate(
        [
            dkeys.reshape(tokens, kv_width).astype(jnp.bfloat16),
            dvalues.reshape(tokens, kv_width).astype(jnp.bfloat16),
        ],
        axis=1,
    )
    every = lax.all_gather(combined, "pipe", axis=0)
    partial_sum = None
    for s in range(n):
        source = lax.rem(pipe + n - s, n)
        theirs = lax.dynamic_index_in_dim(every, source, 0, keepdims=False)
        term = lax.dot_general(
            columns[:, s].reshape(tokens, depth), theirs, (((0,), (0,)), ((), ())),
            preferred_element_type=jnp.float32,
        )
        partial_sum = term if partial_sum is None else partial_sum + term
    total = partial_sum + lax.ppermute(partial_sum, "dp", [(0, 1), (1, 0)])
    return (attended, total[:, :kv_width], total[:, kv_width:])


def solution(mesh):
    placed = (
        P(("pipe", "dp"), None, "tensor"),
        P("tensor"),
        P(("pipe", "dp"), None, "tensor"),
        P("pipe", "tensor"),
        P("pipe", "tensor"),
        P(("pipe", "dp"), None, "tensor"),
    )
    return jax.shard_map(
        functools.partial(shards, mesh.shape["pipe"]),
        mesh=mesh,
        in_specs=placed,
        out_specs=(P(("pipe", "dp"), None, "tensor"), P("pipe", "tensor"), P("pipe", "tensor")),
        check_vma=False,
    )
```

time: 698 us -> 485 us (0.69)
  waiting for transfers between devices: 572 us -> 216 us
  Pallas kernels: 0 us -> 131 us
  other arithmetic: 5.19 us -> 22.1 us
  matrix products: 86.2 us -> 74.1 us
  local copies, waits for them, and re-layouts: 13.9 us -> 21.1 us
    reduce_scatter x1 -> x0, waiting for transfers between devices: 281 us -> none  [shards(): lax.psum_scatter(lax.dot_general(columns, combined, (((0,), (0,)), ((), (...]
    ppermute x0 -> x4, waiting for transfers between devices: none -> 160 us  [the longest x1 82.1 us: shards(): total = partial_sum + lax.ppermute(partial_sum, 'dp', [(0, 1), (1, 0)])]
    pallas_call x0 -> x1, Pallas kernels: none -> 131 us  [gather_all(): pl.pallas_call(functools.partial(gather_kernel, n, hc, wc), out_shape=[ja...]
    all_gather x3 -> x2, waiting for transfers between devices: 186 us -> 55.8 us  [the longest x1 55.8 us: shards(): columns = lax.all_gather(jnp.stack(parts), 'tensor', axis=0)]
    psum x1 -> x0, waiting for transfers between devices: 102 us -> none  [shards(): total = lax.psum(partial_sum, 'dp')]
    dot_general x3 -> x6, matrix products: 28.2 us -> 17 us  [the longest x4 7.54 us: shards(): lax.dot_general(columns[:, s].reshape(tokens, depth), theirs, (((0,), (0,...]
    convert_element_type x1 -> x2, other arithmetic: 0.01 us -> 9.84 us  [the longest x1 9.83 us: shards(): (wide * lax.rsqrt(power + 1e-05) * gains.reshape(-1).astype(jnp.float32))...]
  transfers between devices with their start and end apart: 5 -> 6, of which waited for: 5 -> 4; matrix products, arithmetic and copies ran while one was open for 5% -> 4% of each run, Pallas kernels for 0% -> 0%
where the time goes in v1:
time: 485 us; the launch traced here: 483 us
  waiting for transfers between devices  216 us (45%)
  Pallas kernels  131 us (27%)
  matrix products  74.1 us (15%)
  other arithmetic  22.1 us (5%)
  local copies, waits for them, and re-layouts  21.1 us (4%)
  between operations  14.3 us (3%)
    pallas_call x1, Pallas kernels, gather_all(): pl.pallas_call(functools.partial(gather_kernel, n, hc, wc), out_shape=[ja...  131 us
    ppermute x1, waiting for transfers between devices, shards(): total = partial_sum + lax.ppermute(partial_sum, 'dp', [(0, 1), (1, 0)])  82.1 us
    ppermute x3, waiting for transfers between devices, shards(): block = lax.ppermute(block, 'pipe', [(i, (i + s) % n) for i in range(n)])  78.3 us
    all_gather x1, waiting for transfers between devices, shards(): columns = lax.all_gather(jnp.stack(parts), 'tensor', axis=0)  55.8 us
    dot_general x1, matrix products, shards(): jnp.einsum('hgqk,qhgd->khd', dscores, query_heads, preferred_element_type...  22.6 us
    sub x1, matrix products, shards(): probs = jax.nn.softmax(scores, axis=-1)  10.8 us
    convert_element_type x1, other arithmetic, shards(): (wide * lax.rsqrt(power + 1e-05) * gains.reshape(-1).astype(jnp.float32))...  9.83 us
  transfers between devices with their start and end apart: 6, of which 4 were waited for; matrix products, arithmetic and copies ran while one was open for 4% of the time, Pallas kernels for 0%

profile of v1, /device:TPU:24, one launch (start us, length us, event | category | flops | bytes accessed | tf_op | source)
XLA Modules:
  0.0 483.3 jit_solution(5005105004304373709)
XLA Ops:
  7.3 130.9 %gather_inputs.1 = (bf16[512,8192]{1,0:T(8,128)(2,1)}, bf16[4,16,128]{2,1,0:T(8,128)(2,1)}, bf16[4,2048,256]{2,1,0:T(8,128)(2,1)}, bf16[4,2048,256]{2,1,0:T(8,128)(2,1)}) custom-call(bf16[512,2048]{1,0:T(8,128)(2,1)} %bitcast.124, bf16[16,128]{1,0:T(8,128)(2,1)} %bitcast.136, bf16[2048,256]{1,0:T(8,128)(2,1)} %k_in.1, bf16[2048,256]{1,0:T(8,128)(2,1)} %v_in.1), custom_call_target="tpu_custom_call" | custom-call | tf_op jit(solution)/shard_map/gather_inputs/pallas_call | solution.py:189
  138.2 5.3 %fusion.2 = f32[512]{0:T(512)S(1)} fusion(bf16[512,8192]{1,0:T(8,128)(2,1)} %get-tuple-element.7), kind=kLoop, calls=%fused_computation.4 | loop fusion | flops 12582400 | bytes 8390656 | tf_op jit(solution)/shard_map/reduce_sum | solution.py:217
  143.5 2.7 copy.53
  146.2 9.8 %fusion.4 = bf16[512,8192]{1,0:T(8,128)(2,1)} fusion(bf16[512,8192]{1,0:T(8,128)(2,1)} %get-tuple-element.7, f32[8192]{0:T(1024)S(1)} %convert.1, f32[512]{0:T(512)S(1)} %add_rsqrt_fusion), kind=kLoop, calls=%fused_computation.6 | loop fusion | flops 16777216 | bytes 16812032 | tf_op jit(solution)/shard_map/convert_element_type | solution.py:218
  156.0 7.1 %convolution_convert_fusion = bf16[512,256]{0,1:T(8,128)(2,1)S(1)} fusion(bf16[512,8192]{1,0:T(8,128)(2,1)} %fusion.4, bf16[8192,256]{1,0:T(8,128)(2,1)} %bitcast.138), kind=kOutput, calls=%fused_computation.33 | convolution fusion | flops 2147614720 | bytes 12845056 | tf_op jit(solution)/shard_map/dot_general | solution.py:233
  164.2 2.4 convolution_convert_fusion.1
  166.5 2.9 copy.54
  169.4 8.1 %fusion.58 = f32[2,512,512,8]{2,1,3,0:T(8,128)} fusion(bf16[512,2,128,1]{0,2,3,1:T(8,128)(2,1)S(1)} %bitcast.131, bf16[512,2,8,128]{0,3,2,1:T(8,128)(2,1)S(1)} %bitcast.116), kind=kOutput, calls=%fused_computation.61 | convolution fusion | flops 1073741824 | bytes 19136512 | tf_op jit(solution)/shard_map/qhgd,khd->hgqk/dot_general | solution.py:249
  177.5 10.8 %fusion.57 = (f32[2,8,512]{2,1,0:T(8,128)S(1)}, f32[2,8,512,512]{2,3,1,0:T(8,128)}) fusion(pred[512,512]{0,1:T(8,128)(4,1)S(1)} %iota_compare_fusion, bf16[512,2,128,1]{0,2,3,1:T(8,128)(2,1)S(1)} %bitcast.139, bf16[512,2,8,128]{0,3,2,1:T(8,128)(2,1)} %bitcast.125), kind=kOutput, calls=%fused_computation.60 | convolution fusion | flops 1090519552 | bytes 19431424 | tf_op jit(solution)/shard_map/sub | solution.py:245
  188.3 8.6 %fusion.30 = bf16[2,512,128]{1,2,0:T(8,128)(2,1)S(1)} fusion(bf16[512,2,8,128]{0,3,2,1:T(8,128)(2,1)S(1)} %bitcast.117, f32[2,8,512,512]{2,3,1,0:T(8,128)} %get-tuple-element.31, f32[2,8,512]{2,1,0:T(8,128)S(1)} %get-tuple-element.30), kind=kOutput, calls=%fused_computation.31 | convolution fusion | flops 1082261504 | bytes 19169280 | tf_op jit(solution)/shard_map/hgqk,qhgd->khd/dot_general | solution.py:252
  196.9 22.6 %fusion.33 = bf16[2,512,128]{1,2,0:T(8,128)(2,1)S(1)} fusion(bf16[512,2,8,128]{0,3,2,1:T(8,128)(2,1)} %bitcast.126, f32[2,512,512,8]{2,1,3,0:T(8,128)} %fusion.58, f32[2,8,512,512]{2,3,1,0:T(8,128)} %get-tuple-element.31, f32[2,8,512]{2,1,0:T(8,128)S(1)} %get-tuple-element.30), kind=kOutput, calls=%fused_computation.32 | convolution fusion | flops 1103241728 | bytes 35946496 | tf_op jit(solution)/shard_map/hgqk,qhgd->khd/dot_general | solution.py:255
  220.5 2.9 dynamic-slice_bitcast_fusion
  223.4 2.4 collective-permute-start
  226.4 25.2 %collective-permute-done = bf16[128,2048]{1,0:T(8,128)(2,1)S(1)} collective-permute-done((bf16[128,2048]{1,0:T(8,128)(2,1)S(1)}, bf16[128,2048]{1,0:T(8,128)(2,1)S(1)}, u32[]{:S(2)}, u32[]{:S(2)}) %collective-permute-start) | collective-permute-done | bytes 524320 | tf_op jit(solution)/shard_map/ppermute | solution.py:229
  251.6 53.1 %collective-permute-done.1 = bf16[128,2048]{1,0:T(8,128)(2,1)S(1)} collective-permute-done((bf16[128,2048]{1,0:T(8,128)(2,1)S(1)}, bf16[128,2048]{1,0:T(8,128)(2,1)S(1)}, u32[]{:S(2)}, u32[]{:S(2)}) %collective-permute-start.1) | collective-permute-done | bytes 524320 | tf_op jit(solution)/shard_map/ppermute | solution.py:229
  306.4 3.1 copy.39
  309.5 55.8 %all-gather.5.cloned.1.call-done = bf16[16,128,2048]{2,1,0:T(8,128)(2,1)} async-done(((bf16[4,128,2048]{2,1,0:T(8,128)(2,1)}), bf16[16,128,2048]{2,1,0:T(8,128)(2,1)}) %all-gather.5.cloned.1.call-update) | async-done | bytes 8388624 | tf_op jit(solution)/shard_map/all_gather | solution.py:231
  365.3 3.7 fusion.55
  373.0 3.6 add_add_fusion
  378.1 7.0 %fusion.19 = bf16[2,128,8,512]{3,1,2,0:T(8,128)(2,1)S(1)} fusion(bf16[512,2,128,1]{0,2,3,1:T(8,128)(2,1)S(1)} %bitcast.132, f32[2,8,512,512]{2,3,1,0:T(8,128)} %get-tuple-element.31, f32[2,8,512]{2,1,0:T(8,128)S(1)} %get-tuple-element.30), kind=kOutput, calls=%fused_computation.27 | convolution fusion | flops 1083179008 | bytes 19169280 | tf_op jit(solution)/shard_map/hgqk,khd->qhgd/dot_general | solution.py:247
  385.1 2.4 copy.40
  387.5 82.1 %collective-permute-done.3 = f32[2048,512]{1,0:T(8,128)} collective-permute-done((f32[2048,512]{1,0:T(8,128)}, f32[2048,512]{1,0:T(8,128)}, u32[]{:S(2)}, u32[]{:S(2)}) %collective-permute-start.3) | collective-permute-done | bytes 4194336 | tf_op jit(solution)/shard_map/ppermute | solution.py:273
  469.6 4.5 add.101
  474.1 2.3 fusion.56
  (25 shorter events, 9.7 us)
Async XLA Ops:
  7.2 299.2 %all-gather.7.cloned.1.call-start = ((), (), s32[]{:S(2)}) async-start(), calls=%async_computation.1 | async-start | bytes 2621440 | tf_op jit(solution)/shard_map/all_gather | solution.py:263
  138.2 5.3 %copy-start.2 = (bf16[4,16,128]{2,1,0:T(8,128)(2,1)S(1)}, bf16[4,16,128]{2,1,0:T(8,128)(2,1)}, u32[]{:S(2)}) copy-start(bf16[4,16,128]{2,1,0:T(8,128)(2,1)} %get-tuple-element.8) | copy-start | bytes 49156
  138.2 5.3 %copy-start.1 = (bf16[1,512,2048]{2,1,0:T(8,128)(2,1)S(1)}, bf16[1,512,2048]{2,1,0:T(8,128)(2,1)}, u32[]{:S(2)}) copy-start(bf16[1,512,2048]{2,1,0:T(8,128)(2,1)} %param.8) | copy-start | bytes 6291460
  156.0 7.1 %copy-start = (bf16[512,8192]{1,0:T(8,128)(2,1)S(1)}, bf16[512,8192]{1,0:T(8,128)(2,1)}, u32[]{:S(2)}) copy-start(bf16[512,8192]{1,0:T(8,128)(2,1)} %fusion.4) | copy-start | bytes 25165828
  156.0 8.2 %copy-start.3 = (bf16[4,2048,256]{2,1,0:T(8,128)(2,1)S(1)}, bf16[4,2048,256]{2,1,0:T(8,128)(2,1)}, u32[]{:S(2)}) copy-start(bf16[4,2048,256]{2,1,0:T(8,128)(2,1)} %get-tuple-element.9) | copy-start | bytes 12582916
  220.4 144.9 %all-gather.5.cloned.1.call-start = ((), (), s32[]{:S(2)}) async-start(), calls=%async_computation | async-start | bytes 10485760 | tf_op jit(solution)/shard_map/all_gather | solution.py:231
  223.4 28.2 %collective-permute-start = (bf16[128,2048]{1,0:T(8,128)(2,1)S(1)}, bf16[128,2048]{1,0:T(8,128)(2,1)S(1)}, u32[]{:S(2)}, u32[]{:S(2)}) collective-permute-start(bf16[128,2048]{1,0:T(8,128)(2,1)S(1)} %get-tuple-element.27), channel_id=1, source_target_pairs={{0,8},{8,16},{16,24},{24,0},{1,9},{9,17},{17,25},{25,1},{2,10},{10... | collective-permute-start | bytes 1572872 | tf_op jit(solution)/shard_map/ppermute | solution.py:229
  225.7 79.0 %collective-permute-start.1 = (bf16[128,2048]{1,0:T(8,128)(2,1)S(1)}, bf16[128,2048]{1,0:T(8,128)(2,1)S(1)}, u32[]{:S(2)}, u32[]{:S(2)}) collective-permute-start(bf16[128,2048]{1,0:T(8,128)(2,1)S(1)} %get-tuple-element.26), channel_id=1, source_target_pairs={{0,16},{8,24},{16,0},{24,8},{1,17},{9,25},{17,1},{25,9},{2,18},{10... | collective-permute-start | bytes 1572872 | tf_op jit(solution)/shard_map/ppermute | solution.py:229
  225.7 79.0 %collective-permute-start.2 = (bf16[128,2048]{1,0:T(8,128)(2,1)S(1)}, bf16[128,2048]{1,0:T(8,128)(2,1)S(1)}, u32[]{:S(2)}, u32[]{:S(2)}) collective-permute-start(bf16[128,2048]{1,0:T(8,128)(2,1)S(1)} %get-tuple-element.25), channel_id=1, source_target_pairs={{0,24},{8,0},{16,8},{24,16},{1,25},{9,1},{17,9},{25,17},{2,26},{10... | collective-permute-start | bytes 1572872 | tf_op jit(solution)/shard_map/ppermute | solution.py:229
  376.6 93.1 %collective-permute-start.3 = (f32[2048,512]{1,0:T(8,128)}, f32[2048,512]{1,0:T(8,128)}, u32[]{:S(2)}, u32[]{:S(2)}) collective-permute-start(f32[2048,512]{1,0:T(8,128)} %add_add_fusion), channel_id=1, source_target_pairs={{0,4},{4,0},{1,5},{5,1},{2,6},{6,2},{3,7},{7,3},{8,12},{12,8},{9,1... | collective-permute-start | bytes 12582920 | tf_op jit(solution)/shard_map/ppermute | solution.py:273
Sparse Core Ops, SparseCore 0:
  220.5 83.0 all-gather.6
  306.4 58.8 all-gather.4

commit v2 on v1

--- a/solution.py
+++ b/solution.py
@@ -207,71 +207,188 @@
     )(hidden, gain, key_weight, value_weight)
 
 
+def attention_kernel(
+    n, normed, q_ref, g_ref, k_ref, v_ref, att_ref, x_out, e_out, comb, acc_k, acc_v,
+    loc_sem, z_s, z_r, ac_s, ac_r, sb_s, sb_r, fw_s, fw_r, e_s, e_r,
+):
+    p = lax.axis_index("pipe")
+    d = lax.axis_index("dp")
+    t = lax.axis_index("tensor")
+    a, c = t // 2, t % 2
+    across, sibling = (1 - a) * 2 + c, a * 2 + (1 - c)
+    far = (1 - a) * 2 + (1 - c)
+    tokens = q_ref.shape[0]
+    depth = x_out.shape[2]
+    quarter = tokens // 4
+    scale = 1.0 / HD**0.5
+    local_heads = k_ref.shape[1] // HD
+    group = q_ref.shape[1] // HD // local_heads
+
+    barrier = pltpu.get_barrier_semaphore()
+    for s in range(1, n):
+        pl.semaphore_signal(barrier, inc=1, device_id=(lax.rem(p + s, n), d, t), device_id_type=MESH)
+    for peer in (across, sibling):
+        pl.semaphore_signal(barrier, inc=1, device_id=(p, d, peer), device_id_type=MESH)
+    pl.semaphore_wait(barrier, n + 1)
+
+    def remote(src, dst, ssem, rsem, dev):
+        return pltpu.make_async_remote_copy(
+            src_ref=src, dst_ref=dst, send_sem=ssem, recv_sem=rsem, device_id=dev, device_id_type=MESH
+        )
+
+    def rows(i):
+        return pl.ds(pl.multiple_of(i * quarter, quarter), quarter)
+
+    def cols(i):
+        return pl.ds(pl.multiple_of(i * depth, depth), depth)
+
+    def z_copy(s):
+        dest = lax.rem(p + s, n)
+        return remote(
+            normed.at[rows(t), cols(dest)], x_out.at[s, rows(t)], z_s.at[s], z_r.at[s], (dest, d, t)
+        )
+
+    def share(s, part, ssem, rsem, peer):
+        ref = x_out.at[s, rows(part)]
+        return remote(ref, ref, ssem.at[s], rsem.at[s], (p, d, peer))
+
+    def e_copy(s, j):
+        dest = lax.rem(p + s, n)
+        width = pl.ds(j * HD, HD)
+        return remote(
+            comb.at[:, :, width], e_out.at[:, s, :, width], e_s.at[s, j], e_r.at[s, j], (dest, d, t)
+        )
+
+    def e_local(j):
+        width = pl.ds(j * HD, HD)
+        return pltpu.make_async_copy(comb.at[:, :, width], e_out.at[:, 0, :, width], loc_sem.at[1 + j])
+
+    def pass_on(s):
+        z_copy(s).wait_recv()
+        share(s, t, ac_s, ac_r, across).start()
+        share(s, t, sb_s, sb_r, sibling).start()
+
+    def pass_over(s):
+        share(s, across, ac_s, ac_r, across).wait_recv()
+        share(s, across, fw_s, fw_r, sibling).start()
+
+    for s in range(1, n):
+        z_copy(s).start()
+    own = pltpu.make_async_copy(normed.at[:, cols(p)], x_out.at[0], loc_sem.at[0])
+    own.start()
+
+    blocks = 2
+    size = tokens // blocks
+    nt = (((1,), (1,)), ((), ()))
+    tn = (((0,), (0,)), ((), ()))
+    f32 = jnp.float32
+    for j in range(local_heads):
+        acc_k[...] = jnp.zeros_like(acc_k)
+        acc_v[...] = jnp.zeros_like(acc_v)
+
+        def head(i, carry, j=j):
+            at = pl.ds(pl.multiple_of((j * group + i) * HD, HD), HD)
+            for b in range(blocks):
+                low, high = b * size, (b + 1) * size
+                q = q_ref[low:high, at]
+                g = g_ref[low:high, at]
+                k = k_ref[:high, j * HD : (j + 1) * HD]
+                v = v_ref[:high, j * HD : (j + 1) * HD]
+                scores = lax.dot_general(q, k, nt, preferred_element_type=f32) * scale
+                qpos = low + lax.broadcasted_iota(jnp.int32, scores.shape, 0)
+                kpos = lax.broadcasted_iota(jnp.int32, scores.shape, 1)
+                scores = jnp.where(qpos >= kpos, scores, -1e30)
+                top = jnp.max(scores, axis=-1, keepdims=True)
+                e = jnp.exp(scores - top)
+                probs = e * (1.0 / jnp.sum(e, axis=-1, keepdims=True))
+                low_probs = probs.astype(jnp.bfloat16)
+                att = jnp.dot(low_probs, v, preferred_element_type=f32)
+                att_ref[low:high, at] = att.astype(jnp.bfloat16)
+                dprobs = lax.dot_general(g, v, nt, preferred_element_type=f32)
+                inner = jnp.sum(dprobs * probs, axis=-1, keepdims=True)
+                dscores = (probs * (dprobs - inner) * scale).astype(jnp.bfloat16)
+                acc_v[:high] += lax.dot_general(low_probs, g, tn, preferred_element_type=f32)
+                acc_k[:high] += lax.dot_general(dscores, q, tn, preferred_element_type=f32)
+            return carry
+
+        lax.fori_loop(0, group, head, 0)
+        comb[0, :, j * HD : (j + 1) * HD] = acc_k[...].astype(jnp.bfloat16)
+        comb[1, :, j * HD : (j + 1) * HD] = acc_v[...].astype(jnp.bfloat16)
+        for s in range(1, n):
+            e_copy(s, j).start()
+        e_local(j).start()
+        if j == 0:
+            pass_on(1)
+    for s in range(2, n):
+        pass_on(s)
+        pass_over(s - 1)
+    pass_over(n - 1)
+    own.wait()
+    for j in range(local_heads):
+        e_local(j).wait()
+    for s in range(1, n):
+        share(s, sibling, sb_s, sb_r, sibling).wait_recv()
+        share(s, far, fw_s, fw_r, sibling).wait_recv()
+        z_copy(s).wait_send()
+        share(s, t, ac_s, ac_r, across).wait_send()
+        share(s, t, sb_s, sb_r, sibling).wait_send()
+        share(s, across, fw_s, fw_r, sibling).wait_send()
+        for j in range(local_heads):
+            e_copy(s, j).wait()
+
+
+def attention(n, normed, queries, out_grad, keys, values):
+    tokens, width = queries.shape
+    kv = keys.shape[1]
+    depth = normed.shape[1] // n
+    dma = pltpu.SemaphoreType.DMA
+    hbm = pl.BlockSpec(memory_space=pl.ANY)
+    vmem = pl.BlockSpec(memory_space=pltpu.VMEM)
+    return pl.pallas_call(
+        functools.partial(attention_kernel, n),
+        out_shape=[
+            jax.ShapeDtypeStruct((tokens, width), jnp.bfloat16),
+            jax.ShapeDtypeStruct((n, tokens, depth), jnp.bfloat16),
+            jax.ShapeDtypeStruct((2, n, tokens, kv), jnp.bfloat16),
+        ],
+        in_specs=[hbm] + [vmem] * 4,
+        out_specs=[vmem, hbm, hbm],
+        scratch_shapes=[
+            pltpu.VMEM((2, tokens, kv), jnp.bfloat16),
+            pltpu.VMEM((tokens, HD), jnp.float32),
+            pltpu.VMEM((tokens, HD), jnp.float32),
+            dma((1 + kv // HD,)),
+        ]
+        + [dma((n,))] * 8
+        + [dma((n, kv // HD))] * 2,
+        compiler_params=pltpu.CompilerParams(
+            collective_id=1, has_side_effects=True, vmem_limit_bytes=44 * 2**20
+        ),
+        name="attention_and_exchange",
+    )(normed, queries, out_grad, keys, values)
+
+
 def shards(n, hidden_in, norm_gain, queries, key_weight, value_weight, out_grad):
-    scale = 1.0 / HD**0.5
-    pipe = lax.axis_index("pipe")
-    tensor = lax.axis_index("tensor")
     depth, kv_width = key_weight.shape
     whole, gains, all_key, all_value = gather_all(n, hidden_in[0], norm_gain, key_weight, value_weight)
     wide = whole.astype(jnp.float32)
     power = jnp.mean(wide * wide, axis=-1, keepdims=True)
     normed = (wide * lax.rsqrt(power + 1e-05) * gains.reshape(-1).astype(jnp.float32)).astype(jnp.bfloat16)
-    tokens = normed.shape[0]
-    local_heads = kv_width // HD
-
-    quarter = tokens // 4
-    mine = lax.dynamic_slice_in_dim(normed, tensor * quarter, quarter, 0)
-    parts = []
-    for s in range(n):
-        dest = lax.rem(pipe + s, n)
-        block = lax.dynamic_slice_in_dim(mine, dest * depth, depth, 1)
-        if s:
-            block = lax.ppermute(block, "pipe", [(i, (i + s) % n) for i in range(n)])
-        parts.append(block)
-    columns = lax.all_gather(jnp.stack(parts), "tensor", axis=0)
-
     keys = jnp.dot(normed, all_key.reshape(-1, kv_width), preferred_element_type=jnp.float32)
     values = jnp.dot(normed, all_value.reshape(-1, kv_width), preferred_element_type=jnp.float32)
-    keys = keys.astype(jnp.bfloat16).reshape(tokens, local_heads, HD)
-    values = values.astype(jnp.bfloat16).reshape(tokens, local_heads, HD)
-    query_heads = queries[0].reshape(tokens, local_heads, GROUP, HD)
-    grad_heads = out_grad[0].reshape(tokens, local_heads, GROUP, HD)
-    scores = (
-        jnp.einsum("qhgd,khd->hgqk", query_heads, keys, preferred_element_type=jnp.float32) * scale
+    attended, columns, every = attention(
+        n, normed, queries[0], out_grad[0], keys.astype(jnp.bfloat16), values.astype(jnp.bfloat16)
     )
-    position = jnp.arange(tokens, dtype=jnp.int32)
-    visible = position[:, None] >= position[None, :]
-    scores = jnp.where(visible, scores, -1e30)
-    probs = jax.nn.softmax(scores, axis=-1)
-    probs_low = probs.astype(jnp.bfloat16)
-    attended = jnp.einsum("hgqk,khd->qhgd", probs_low, values, preferred_element_type=jnp.float32)
-    attended = attended.reshape(1, tokens, local_heads * GROUP * HD).astype(jnp.bfloat16)
-    dprobs = jnp.einsum("qhgd,khd->hgqk", grad_heads, values, preferred_element_type=jnp.float32)
-    inner = jnp.sum(dprobs * probs, axis=-1, keepdims=True)
-    dscores = (probs * (dprobs - inner) * scale).astype(jnp.bfloat16)
-    dvalues = jnp.einsum(
-        "hgqk,qhgd->khd", probs_low, grad_heads, preferred_element_type=jnp.float32
-    )
-    dkeys = jnp.einsum("hgqk,qhgd->khd", dscores, query_heads, preferred_element_type=jnp.float32)
-    combined = jnp.concatenate(
-        [
-            dkeys.reshape(tokens, kv_width).astype(jnp.bfloat16),
-            dvalues.reshape(tokens, kv_width).astype(jnp.bfloat16),
-        ],
-        axis=1,
-    )
-    every = lax.all_gather(combined, "pipe", axis=0)
-    partial_sum = None
-    for s in range(n):
-        source = lax.rem(pipe + n - s, n)
-        theirs = lax.dynamic_index_in_dim(every, source, 0, keepdims=False)
+    columns = columns.reshape(-1, depth)
+    swap = [(0, 1), (1, 0)]
+    grads = []
+    for i in range(2):
         term = lax.dot_general(
-            columns[:, s].reshape(tokens, depth), theirs, (((0,), (0,)), ((), ())),
+            columns, every[i].reshape(-1, kv_width), (((0,), (0,)), ((), ())),
             preferred_element_type=jnp.float32,
         )
-        partial_sum = term if partial_sum is None else partial_sum + term
-    total = partial_sum + lax.ppermute(partial_sum, "dp", [(0, 1), (1, 0)])
-    return (attended, total[:, :kv_width], total[:, kv_width:])
+        grads.append(term + lax.ppermute(term, "dp", swap))
+    return (attended[None], grads[0], grads[1])
 
 
 def solution(mesh):

time: 485 us -> 352 us (0.73)
  waiting for transfers between devices: 216 us -> 85.4 us
  Pallas kernels: 131 us -> 225 us
  matrix products: 74.1 us -> 17 us
  local copies, waits for them, and re-layouts: 21.1 us -> 2.55 us
  between operations: 14.3 us -> 0.79 us
    pallas_call x0 -> x1, Pallas kernels: none -> 94.2 us  [attention(): pl.pallas_call(functools.partial(attention_kernel, n), out_shape=[jax.Sha...]
    ppermute x4 -> x2, waiting for transfers between devices: 160 us -> 85.4 us  [shards(): grads.append(term + lax.ppermute(term, 'dp', swap))]
    all_gather x2 -> x0, waiting for transfers between devices: 55.8 us -> none  [the longest x1 55.8 us: shards(): columns = lax.all_gather(jnp.stack(parts), 'tensor', axis=0)]
    dot_general x8 -> x2, matrix products: 53.9 us -> 8.74 us  [shards(): lax.dot_general(columns, every[i].reshape(-1, kv_width), (((0,), (0,)), (...]
    sub x1 -> x0, matrix products: 10.8 us -> none  [shards(): probs = jax.nn.softmax(scores, axis=-1)]
    another operation x3 -> x0, local copies, waits for them, and re-layouts: 8.43 us -> none  [the longest x1 2.88 us: shards(): columns = lax.all_gather(jnp.stack(parts), 'tensor', axis=0)]
    slice x2 -> x1, local copies, waits for them, and re-layouts: 6.09 us -> 0.14 us  [shards(): every[i].reshape(-1, kv_width)]
  transfers between devices with their start and end apart: 6 -> 2, of which waited for: 4 -> 2; matrix products, arithmetic and copies ran while one was open for 4% -> 1% of each run, Pallas kernels for 0% -> 0%
where the time goes in v2:
time: 352 us; the launch traced here: 351 us
  Pallas kernels  225 us (64%)
  waiting for transfers between devices  85.4 us (24%)
  other arithmetic  18.3 us (5%)
  matrix products  17 us (5%)
    pallas_call x1, Pallas kernels, gather_all(): pl.pallas_call(functools.partial(gather_kernel, n, hc, wc), out_shape=[ja...  131 us
    pallas_call x1, Pallas kernels, attention(): pl.pallas_call(functools.partial(attention_kernel, n), out_shape=[jax.Sha...  94.2 us
    ppermute x2, waiting for transfers between devices, shards(): grads.append(term + lax.ppermute(term, 'dp', swap))  85.4 us
    convert_element_type x1, other arithmetic, shards(): (wide * lax.rsqrt(power + 1e-05) * gains.reshape(-1).astype(jnp.float32))...  10 us
    dot_general x2, matrix products, shards(): lax.dot_general(columns, every[i].reshape(-1, kv_width), (((0,), (0,)), (...  8.74 us
  transfers between devices with their start and end apart: 2, of which 2 were waited for; matrix products, arithmetic and copies ran while one was open for 1% of the time, Pallas kernels for 0%

profile of v2, /device:TPU:24, one launch (start us, length us, event | category | flops | bytes accessed | tf_op | source)
XLA Modules:
  0.0 351.4 jit_solution(8275354429223982310)
XLA Ops:
  0.6 130.9 %gather_inputs.1 = (bf16[512,8192]{1,0:T(8,128)(2,1)}, bf16[4,16,128]{2,1,0:T(8,128)(2,1)}, bf16[4,2048,256]{2,1,0:T(8,128)(2,1)}, bf16[4,2048,256]{2,1,0:T(8,128)(2,1)}) custom-call(bf16[512,2048]{1,0:T(8,128)(2,1)} %bitcast.25, bf16[16,128]{1,0:T(8,128)(2,1)} %bitcast.29, bf16[2048,256]{1,0:T(8,128)(2,1)} %k_in.1, bf16[2048,256]{1,0:T(8,128)(2,1)} %v_in.1), custom_call_target="tpu_custom_call" | custom-call | tf_op jit(solution)/shard_map/gather_inputs/pallas_call | solution.py:189
  131.5 0.0 copy-start.2
  131.5 5.1 %fusion = f32[512]{0:T(512)S(1)} fusion(bf16[512,8192]{1,0:T(8,128)(2,1)} %get-tuple-element.10), kind=kLoop, calls=%fused_computation.2 | loop fusion | flops 12582400 | bytes 8390656 | tf_op jit(solution)/shard_map/reduce_sum | solution.py:375
  136.6 0.0 copy-done.2
  136.7 10.0 %fusion.2.normed = bf16[512,8192]{1,0:T(8,128)(2,1)} fusion(bf16[512,8192]{1,0:T(8,128)(2,1)} %get-tuple-element.10, f32[8192]{0:T(1024)S(1)} %convert.1, f32[512]{0:T(512)S(1)} %add_rsqrt_fusion), kind=kLoop, calls=%fused_computation.4 | loop fusion | flops 16777216 | bytes 16812032 | tf_op jit(solution)/shard_map/convert_element_type | solution.py:376
  146.7 0.0 copy-done.4
  146.7 5.9 %convolution_convert_fusion.v_ref = bf16[512,256]{1,0:T(8,128)(2,1)S(1)} fusion(bf16[512,8192]{1,0:T(8,128)(2,1)} %fusion.2.normed, bf16[8192,256]{1,0:T(8,128)(2,1)S(1)} %bitcast.35), kind=kOutput, calls=%fused_computation.5 | convolution fusion | flops 2147614720 | bytes 12845056 | tf_op jit(solution)/shard_map/dot_general | solution.py:378
  152.6 0.0 copy-start
  152.6 0.0 copy-start.1
  152.7 1.1 slice-done.1
  153.7 2.3 convolution_convert_fusion.1.k_ref
  156.1 94.2 %attention_and_exchange.1 = (bf16[512,2048]{1,0:T(8,128)(2,1)S(1)}, bf16[4,512,2048]{2,1,0:T(8,128)(2,1)}, bf16[2,4,512,256]{3,2,1,0:T(8,128)(2,1)S(1)}) custom-call(bf16[512,8192]{1,0:T(8,128)(2,1)} %fusion.2.normed, bf16[512,2048]{1,0:T(8,128)(2,1)S(1)} %bitcast.20, bf16[512,2048]{1,0:T(8,128)(2,1)S(1)} %bitcast.21, ...), custom_call_target="tpu_custom_call" | custom-call | tf_op jit(solution)/shard_map/attention_and_exchange/pallas_call | solution.py:347
  250.3 0.0 slice-start.2
  250.3 0.1 fusion.3
  250.5 0.0 slice-start.3
  250.5 6.1 %fusion.5 = f32[2048,256]{1,0:T(8,128)S(1)} fusion(bf16[2048,2048]{1,0:T(8,128)(2,1)} %bitcast.30, bf16[2048,256]{1,0:T(8,128)(2,1)S(1)} %bitcast.27), kind=kOutput, calls=%fused_computation.10 | convolution fusion | flops 2147483648 | bytes 11534336 | tf_op jit(solution)/shard_map/dot_general | solution.py:386
  256.6 1.6 collective-permute-start.1
  258.2 2.6 fusion.4
  260.8 0.6 collective-permute-start
  261.4 43.9 %collective-permute-done.1 = f32[2048,256]{1,0:T(8,128)S(1)} collective-permute-done((f32[2048,256]{1,0:T(8,128)S(1)}, f32[2048,256]{1,0:T(8,128)S(1)}, u32[]{:S(2)}, u32[]{:S(2)}) %collective-permute-start.1) | collective-permute-done | bytes 2097184 | tf_op jit(solution)/shard_map/ppermute | solution.py:390
  305.3 1.6 add.20
  306.9 41.6 %collective-permute-done = f32[2048,256]{1,0:T(8,128)S(1)} collective-permute-done((f32[2048,256]{1,0:T(8,128)S(1)}, f32[2048,256]{1,0:T(8,128)S(1)}, u32[]{:S(2)}, u32[]{:S(2)}) %collective-permute-start) | collective-permute-done | bytes 2097184 | tf_op jit(solution)/shard_map/ppermute | solution.py:390
  348.4 1.6 add.19
  350.0 1.3 copy.10
  (14 shorter events, 0.0 us)
Async XLA Ops:
  131.5 5.1 %copy-start.2 = (bf16[4,16,128]{2,1,0:T(8,128)(2,1)S(1)}, bf16[4,16,128]{2,1,0:T(8,128)(2,1)}, u32[]{:S(2)}) copy-start(bf16[4,16,128]{2,1,0:T(8,128)(2,1)} %get-tuple-element.11) | copy-start | bytes 49156
  136.7 10.0 %copy-start.4 = (bf16[4,2048,256]{2,1,0:T(8,128)(2,1)S(1)}, bf16[4,2048,256]{2,1,0:T(8,128)(2,1)}, u32[]{:S(2)}) copy-start(bf16[4,2048,256]{2,1,0:T(8,128)(2,1)} %get-tuple-element.13) | copy-start | bytes 12582916
  146.7 6.0 %slice-start = ((s8[8388608]{0:T(1024)(128)(4,1)}), s8[4194304]{0:T(1024)(128)(4,1)S(1)}, s32[]{:S(2)}) async-start(s8[8388608]{0:T(1024)(128)(4,1)} %bitcast.23), calls=%async_computation | async-start | bytes 8388608
  146.7 6.0 %copy-start.3 = (bf16[4,2048,256]{2,1,0:T(8,128)(2,1)S(1)}, bf16[4,2048,256]{2,1,0:T(8,128)(2,1)}, u32[]{:S(2)}) copy-start(bf16[4,2048,256]{2,1,0:T(8,128)(2,1)} %get-tuple-element.12) | copy-start | bytes 12582916
  146.7 7.0 %slice-start.1 = ((s8[8388608]{0:T(1024)(128)(4,1)}), s8[4194304]{0:T(1024)(128)(4,1)S(1)}, s32[]{:S(2)}) async-start(s8[8388608]{0:T(1024)(128)(4,1)} %bitcast.23), calls=%async_computation.1 | async-start | bytes 8388608
  152.6 3.4 copy-start
  152.6 3.4 copy-start.1
  250.3 7.9 %slice-start.2 = ((s8[8388608]{0:T(1024)(128)(4,1)}), s8[4194304]{0:T(1024)(128)(4,1)S(1)}, s32[]{:S(2)}) async-start(s8[8388608]{0:T(1024)(128)(4,1)} %bitcast.31), calls=%async_computation.2 | async-start | bytes 8388608
  250.5 7.7 %slice-start.3 = ((s8[8388608]{0:T(1024)(128)(4,1)}), s8[4194304]{0:T(1024)(128)(4,1)S(1)}, s32[]{:S(2)}) async-start(s8[8388608]{0:T(1024)(128)(4,1)} %bitcast.31), calls=%async_computation.3 | async-start | bytes 8388608
  256.6 48.6 %collective-permute-start.1 = (f32[2048,256]{1,0:T(8,128)S(1)}, f32[2048,256]{1,0:T(8,128)S(1)}, u32[]{:S(2)}, u32[]{:S(2)}) collective-permute-start(f32[2048,256]{1,0:T(8,128)S(1)} %fusion.5), channel_id=1, source_target_pairs={{0,4},{4,0},{1,5},{5,1},{2,6},{6,2},{3,7},{7,3},{8,12},{12,8},{9,1... | collective-permute-start | bytes 6291464 | tf_op jit(solution)/shard_map/ppermute | solution.py:390
  260.8 87.6 %collective-permute-start = (f32[2048,256]{1,0:T(8,128)S(1)}, f32[2048,256]{1,0:T(8,128)S(1)}, u32[]{:S(2)}, u32[]{:S(2)}) collective-permute-start(f32[2048,256]{1,0:T(8,128)S(1)} %fusion.4), channel_id=1, source_target_pairs={{0,4},{4,0},{1,5},{5,1},{2,6},{6,2},{3,7},{7,3},{8,12},{12,8},{9,1... | collective-permute-start | bytes 6291464 | tf_op jit(solution)/shard_map/ppermute | solution.py:390

commit v3 on v2

--- a/solution.py
+++ b/solution.py
@@ -12,8 +12,8 @@
 
 
 def gather_kernel(
-    n, hc, wc, h_in, g_in, k_in, v_in, h_out, g_out, k_out, v_out,
-    loc_sem, hx_s, hx_r, hs_s, hs_r, hf_s, hf_r, g_s, g_r, zu_s, zd_s, z_r, y_s, y_r,
+    n, wc, g_in, k_in, v_in, g_out, k_out, v_out,
+    loc_sem, g_s, g_r, zu_s, zd_s, z_r, y_s, y_r,
 ):
     p = lax.axis_index("pipe")
     d = lax.axis_index("dp")
@@ -21,11 +21,9 @@
     a, c = t // 2, t % 2
     across, sibling = (1 - a) * 2 + c, a * 2 + (1 - c)
     far = (1 - a) * 2 + (1 - c)
-    rows, width = h_in.shape
     depth = k_in.shape[0]
     half = depth // 2
     piece = half // wc
-    hrows = rows // hc
 
     barrier = pltpu.get_barrier_semaphore()
     for peer in (across, sibling, far):
@@ -39,26 +37,6 @@
     def remote(src, dst, ssem, rsem, dev):
         return pltpu.make_async_remote_copy(
             src_ref=src, dst_ref=dst, send_sem=ssem, recv_sem=rsem, device_id=dev, device_id_type=MESH
-        )
-
-    def cols(i):
-        return pl.ds(pl.multiple_of(i * width, width), width)
-
-    def hslice(ref, i, k):
-        return ref.at[pl.ds(k * hrows, hrows), cols(i)]
-
-    def hown(k):
-        return h_in.at[pl.ds(k * hrows, hrows)]
-
-    def x_copy(k, owner):
-        return remote(hown(k), hslice(h_out, owner, k), hx_s.at[k], hx_r.at[k], (p, d, across))
-
-    def sib_copy(k, owner):
-        return remote(hown(k), hslice(h_out, owner, k), hs_s.at[k], hs_r.at[k], (p, d, sibling))
-
-    def fwd_copy(k, owner):
-        return remote(
-            hslice(h_out, owner, k), hslice(h_out, owner, k), hf_s.at[k], hf_r.at[k], (p, d, sibling)
         )
 
     def wpart(ref, b, k, hd):
@@ -95,24 +73,14 @@
     ]
     for copy in gains:
         copy.start()
-    for k in range(hc):
-        x_copy(k, t).start()
-    for k in range(hc):
-        sib_copy(k, t).start()
     local = [
-        pltpu.make_async_copy(h_in, h_out.at[:, cols(t)], loc_sem.at[0]),
-        pltpu.make_async_copy(g_in, g_out.at[t], loc_sem.at[1]),
-        pltpu.make_async_copy(k_in, k_out.at[p], loc_sem.at[2]),
-        pltpu.make_async_copy(v_in, v_out.at[p], loc_sem.at[3]),
+        pltpu.make_async_copy(g_in, g_out.at[t], loc_sem.at[0]),
+        pltpu.make_async_copy(k_in, k_out.at[p], loc_sem.at[1]),
+        pltpu.make_async_copy(v_in, v_out.at[p], loc_sem.at[2]),
     ]
     for copy in local:
         copy.start()
 
-    def hidden_step(k):
-        x_copy(k, across).wait_recv()
-        fwd_copy(k, across).start()
-
-    done = 0
     for s in range(1, n):
         for k in range(2 * wc):
 
@@ -138,11 +106,6 @@
 
                 y_copy(b, k, d).start()
 
-        goal = hc if s == n - 1 else min(hc, (hc * s) // (n - 1))
-        while done < goal:
-            hidden_step(done)
-            done += 1
-
     for s in range(1, n):
         for k in range(2 * wc):
             for up in (True, False):
@@ -164,12 +127,6 @@
             def _(s=s, k=k):
                 z_copy(wsrc(k), p + s, k, False).wait_send()
 
-    for k in range(hc):
-        sib_copy(k, sibling).wait_recv()
-        fwd_copy(k, far).wait_recv()
-        x_copy(k, t).wait_send()
-        sib_copy(k, t).wait_send()
-        fwd_copy(k, across).wait_send()
     for i, peer in enumerate((across, sibling, far)):
         remote(g_in, g_out.at[peer], g_s.at[i], g_r.at[i], (p, d, peer)).wait_recv()
     for copy in gains:
@@ -178,33 +135,30 @@
         copy.wait()
 
 
-def gather_all(n, hidden, gain, key_weight, value_weight):
-    rows, width = hidden.shape
+def gather_weights(n, gain, key_weight, value_weight):
     depth, kv = key_weight.shape
     gain = gain.reshape(-1, 128)
-    hc = 4
     wc = 2 if n <= 8 else 1
     dma = pltpu.SemaphoreType.DMA
     any_spec = pl.BlockSpec(memory_space=pl.ANY)
     return pl.pallas_call(
-        functools.partial(gather_kernel, n, hc, wc),
+        functools.partial(gather_kernel, n, wc),
         out_shape=[
-            jax.ShapeDtypeStruct((rows, 4 * width), hidden.dtype),
             jax.ShapeDtypeStruct((4,) + gain.shape, gain.dtype),
             jax.ShapeDtypeStruct((n, depth, kv), key_weight.dtype),
             jax.ShapeDtypeStruct((n, depth, kv), value_weight.dtype),
         ],
-        in_specs=[any_spec] * 4,
-        out_specs=[any_spec] * 4,
+        in_specs=[any_spec] * 3,
+        out_specs=[any_spec] * 3,
         scratch_shapes=[
-            dma((4,)),
-            dma((hc,)), dma((hc,)), dma((hc,)), dma((hc,)), dma((hc,)), dma((hc,)),
+            dma((3,)),
             dma((3,)), dma((3,)),
             dma((n, 2 * wc)), dma((n, 2 * wc)), dma((n, 2 * wc)), dma((n, 2 * wc)), dma((n, 2 * wc)),
         ],
         compiler_params=pltpu.CompilerParams(collective_id=0, has_side_effects=True),
-        name="gather_inputs",
-    )(hidden, gain, key_weight, value_weight)
+        name="gather_weights",
+        cost_estimate=pl.CostEstimate(flops=8 * 10**10, bytes_accessed=2 * 10**8, transcendentals=0),
+    )(gain, key_weight, value_weight)
 
 
 def attention_kernel(
@@ -370,7 +324,8 @@
 
 def shards(n, hidden_in, norm_gain, queries, key_weight, value_weight, out_grad):
     depth, kv_width = key_weight.shape
-    whole, gains, all_key, all_value = gather_all(n, hidden_in[0], norm_gain, key_weight, value_weight)
+    whole = lax.all_gather(hidden_in[0], "tensor", axis=1, tiled=True)
+    gains, all_key, all_value = gather_weights(n, norm_gain, key_weight, value_weight)
     wide = whole.astype(jnp.float32)
     power = jnp.mean(wide * wide, axis=-1, keepdims=True)
     normed = (wide * lax.rsqrt(power + 1e-05) * gains.reshape(-1).astype(jnp.float32)).astype(jnp.bfloat16)
@@ -387,7 +342,9 @@
             columns, every[i].reshape(-1, kv_width), (((0,), (0,)), ((), ())),
             preferred_element_type=jnp.float32,
         )
-        grads.append(term + lax.ppermute(term, "dp", swap))
+        term = lax.reduce_precision(term, 8, 7)
+        other = lax.ppermute(term.astype(jnp.bfloat16), "dp", swap)
+        grads.append(term + other.astype(jnp.float32))
     return (attended[None], grads[0], grads[1])
 
 

time: 352 us -> 275 us (0.78)
  Pallas kernels: 225 us -> 177 us
  waiting for transfers between devices: 85.4 us -> 42.3 us
  between operations: 0.79 us -> 14.1 us
    pallas_call x1, Pallas kernels: 131 us -> 79.3 us  [gather_weights(): pl.pallas_call(functools.partial(gather_kernel, n, wc), out_shape=[jax.Sh...]
    ppermute x2, waiting for transfers between devices: 85.4 us -> 41.7 us  [shards(): other = lax.ppermute(term.astype(jnp.bfloat16), 'dp', swap)]
  transfers between devices with their start and end apart: 2 -> 3, of which waited for: 2 -> 2; matrix products, arithmetic and copies ran while one was open for 1% -> 2% of each run, Pallas kernels for 0% -> 29%
where the time goes in v3:
time: 275 us
  Pallas kernels  177 us (64%)
  waiting for transfers between devices  42.3 us (15%)
  other arithmetic  18.7 us (7%)
  matrix products  18.2 us (7%)
  between operations  14.1 us (5%)
    pallas_call x1, Pallas kernels, attention(): pl.pallas_call(functools.partial(attention_kernel, n), out_shape=[jax.Sha...  97.5 us
    pallas_call x1, Pallas kernels, gather_weights(): pl.pallas_call(functools.partial(gather_kernel, n, wc), out_shape=[jax.Sh...  79.3 us
    ppermute x2, waiting for transfers between devices, shards(): other = lax.ppermute(term.astype(jnp.bfloat16), 'dp', swap)  41.7 us
    convert_element_type x1, other arithmetic, shards(): (wide * lax.rsqrt(power + 1e-05) * gains.reshape(-1).astype(jnp.float32))...  9.86 us
    dot_general x2, matrix products, shards(): lax.dot_general(columns, every[i].reshape(-1, kv_width), (((0,), (0,)), (...  8.78 us
    dot_general x1, matrix products, shards(): jnp.dot(normed, all_value.reshape(-1, kv_width), preferred_element_type=j...  7.05 us
  transfers between devices with their start and end apart: 3, of which 2 were waited for; matrix products, arithmetic and copies ran while one was open for 2% of the time, Pallas kernels for 29%

profile of v3, /device:TPU:24, one launch (start us, length us, event | category | flops | bytes accessed | tf_op | source)
XLA Modules:
  0.0 274.9 jit_solution(53426276492484094)
XLA Ops:
  7.2 0.0 all-gather.3.cloned.1.call-start
  7.2 0.7 all-gather.3.cloned.1.call-update
  7.9 79.3 %gather_weights.1 = (bf16[4,16,128]{2,1,0:T(8,128)(2,1)}, bf16[4,2048,256]{2,1,0:T(8,128)(2,1)}, bf16[4,2048,256]{2,1,0:T(8,128)(2,1)}) custom-call(bf16[16,128]{1,0:T(8,128)(2,1)} %bitcast.33, bf16[2048,256]{1,0:T(8,128)(2,1)} %k_in.1, bf16[2048,256]{1,0:T(8,128)(2,1)} %v_in.1), custom_call_target="tpu_custom_call" | custom-call | flops 80000000000 | bytes 200000000 | tf_op jit(solution)/shard_map/gather_weights/pallas_call | solution.py:144
  87.2 0.7 convert.2
  87.9 5.1 %fusion = f32[512]{0:T(512)S(1)} fusion(bf16[1,512,8192]{2,1,0:T(8,128)(2,1)} %all-gather.3.cloned.1.call-done), kind=kLoop, calls=%fused_computation.2 | loop fusion | flops 12582400 | bytes 8390656 | tf_op jit(solution)/shard_map/reduce_sum | solution.py:330
  93.1 9.9 %fusion.2.normed = bf16[512,8192]{1,0:T(8,128)(2,1)} fusion(bf16[1,512,8192]{2,1,0:T(8,128)(2,1)} %all-gather.3.cloned.1.call-done, f32[8192]{0:T(1024)S(1)} %convert.2, f32[512]{0:T(512)S(1)} %add_rsqrt_fusion), kind=kLoop, calls=%fused_computation.4 | loop fusion | flops 16777216 | bytes 16812032 | tf_op jit(solution)/shard_map/convert_element_type | solution.py:331
  102.9 7.0 %convolution_convert_fusion.v_ref = bf16[512,256]{1,0:T(8,128)(2,1)S(1)} fusion(bf16[512,8192]{1,0:T(8,128)(2,1)} %fusion.2.normed, bf16[8192,256]{1,0:T(8,128)(2,1)} %bitcast.35), kind=kOutput, calls=%fused_computation.9 | convolution fusion | flops 2147614720 | bytes 12845056 | tf_op jit(solution)/shard_map/dot_general | solution.py:333
  110.0 0.0 copy-done.2
  110.0 1.1 copy-done.3
  111.1 2.3 convolution_convert_fusion.1.k_ref
  113.4 97.5 %attention_and_exchange.1 = (bf16[512,2048]{1,0:T(8,128)(2,1)S(1)}, bf16[4,512,2048]{2,1,0:T(8,128)(2,1)}, bf16[2,4,512,256]{3,2,1,0:T(8,128)(2,1)S(1)}) custom-call(bf16[512,8192]{1,0:T(8,128)(2,1)} %fusion.2.normed, bf16[512,2048]{1,0:T(8,128)(2,1)S(1)} %bitcast.23, bf16[512,2048]{1,0:T(8,128)(2,1)S(1)} %bitcast.24, ...), custom_call_target="tpu_custom_call" | custom-call | tf_op jit(solution)/shard_map/attention_and_exchange/pallas_call | solution.py:301
  210.9 0.0 slice-start
  210.9 0.1 fusion.3
  211.1 0.0 slice-start.1
  211.1 6.2 %fusion.4 = (bf16[2048,256]{1,0:T(8,128)(2,1)S(1)}, f32[2048,256]{1,0:T(8,128)S(1)}) fusion(bf16[2048,2048]{1,0:T(8,128)(2,1)} %bitcast.29, bf16[2048,256]{1,0:T(8,128)(2,1)S(1)} %bitcast.27), kind=kOutput, calls=%fused_computation.13 | convolution fusion | flops 2148532224 | bytes 12582912 | tf_op jit(solution)/shard_map/dot_general | solution.py:341
  217.2 0.6 collective-permute-start
  217.8 0.0 slice-done.1
  217.8 2.6 fusion.5
  220.5 1.6 collective-permute-start.1
  222.1 21.3 %collective-permute-done = bf16[2048,256]{1,0:T(8,128)(2,1)S(1)} collective-permute-done((bf16[2048,256]{1,0:T(8,128)(2,1)S(1)}, bf16[2048,256]{1,0:T(8,128)(2,1)S(1)}, u32[]{:S(2)}, u32[]{:S(2)}) %collective-permute-start) | collective-permute-done | bytes 1048608 | tf_op jit(solution)/shard_map/ppermute | solution.py:346
  243.3 1.5 convert_add_fusion.1
  244.8 20.4 %collective-permute-done.1 = bf16[2048,256]{1,0:T(8,128)(2,1)S(1)} collective-permute-done((bf16[2048,256]{1,0:T(8,128)(2,1)S(1)}, bf16[2048,256]{1,0:T(8,128)(2,1)S(1)}, u32[]{:S(2)}, u32[]{:S(2)}) %collective-permute-start.1) | collective-permute-done | bytes 1048608 | tf_op jit(solution)/shard_map/ppermute | solution.py:346
  265.2 1.5 convert_add_fusion
  266.8 1.3 copy.10
  (10 shorter events, 0.0 us)
Async XLA Ops:
  7.2 80.8 %all-gather.3.cloned.1.call-start = ((), (), s32[]{:S(2)}) async-start(), calls=%async_computation | async-start | bytes 10485760 | tf_op jit(solution)/shard_map/all_gather | solution.py:327
  102.9 7.1 %copy-start.2 = (bf16[512,8192]{1,0:T(8,128)(2,1)S(1)}, bf16[512,8192]{1,0:T(8,128)(2,1)}, u32[]{:S(2)}) copy-start(bf16[512,8192]{1,0:T(8,128)(2,1)} %fusion.2.normed) | copy-start | bytes 25165828
  102.9 8.2 %copy-start.3 = (bf16[4,2048,256]{2,1,0:T(8,128)(2,1)S(1)}, bf16[4,2048,256]{2,1,0:T(8,128)(2,1)}, u32[]{:S(2)}) copy-start(bf16[4,2048,256]{2,1,0:T(8,128)(2,1)} %get-tuple-element.10) | copy-start | bytes 12582916
  111.1 2.3 copy-start
  111.1 2.3 copy-start.1
  210.9 6.9 %slice-start = ((s8[8388608]{0:T(1024)(128)(4,1)}), s8[4194304]{0:T(1024)(128)(4,1)S(1)}, s32[]{:S(2)}) async-start(s8[8388608]{0:T(1024)(128)(4,1)} %bitcast.30), calls=%async_computation.1 | async-start | bytes 8388608
  211.1 6.8 %slice-start.1 = ((s8[8388608]{0:T(1024)(128)(4,1)}), s8[4194304]{0:T(1024)(128)(4,1)S(1)}, s32[]{:S(2)}) async-start(s8[8388608]{0:T(1024)(128)(4,1)} %bitcast.30), calls=%async_computation.2 | async-start | bytes 8388608
  217.2 26.1 %collective-permute-start = (bf16[2048,256]{1,0:T(8,128)(2,1)S(1)}, bf16[2048,256]{1,0:T(8,128)(2,1)S(1)}, u32[]{:S(2)}, u32[]{:S(2)}) collective-permute-start(bf16[2048,256]{1,0:T(8,128)(2,1)S(1)} %get-tuple-element.17), channel_id=1, source_target_pairs={{0,4},{4,0},{1,5},{5,1},{2,6},{6,2},{3,7},{7,3},{8,12},{12,8},{9,1... | collective-permute-start | bytes 3145736 | tf_op jit(solution)/shard_map/ppermute | solution.py:346
  220.5 44.8 %collective-permute-start.1 = (bf16[2048,256]{1,0:T(8,128)(2,1)S(1)}, bf16[2048,256]{1,0:T(8,128)(2,1)S(1)}, u32[]{:S(2)}, u32[]{:S(2)}) collective-permute-start(bf16[2048,256]{1,0:T(8,128)(2,1)S(1)} %get-tuple-element.19), channel_id=1, source_target_pairs={{0,4},{4,0},{1,5},{5,1},{2,6},{6,2},{3,7},{7,3},{8,12},{12,8},{9,1... | collective-permute-start | bytes 3145736 | tf_op jit(solution)/shard_map/ppermute | solution.py:346
Sparse Core Ops, SparseCore 0:
  9.6 59.2 all-gather.2
